TPU v7x, 512 devices: a whole 4x8x8 slice. The times are simulated.
512 devices in a mesh: blk: 64 (over x, z_hi, y), width: 8 (over z_lo, core).
Axes of the slice: x: 4, y: 8, z: 8 (z_hi: 2, z_lo: 4; z = z_hi * 4 + z_lo), core: 2. Of those that a mesh axis runs over, the one named last changes fastest.
Arguments:
- tokens: bfloat16 [352, 8192], P(None, ('width', 'blk')), may hold values from -6 to 6
- gate_weight: bfloat16 [8192, 16384], P('width', 'blk'), may hold values from -0.0625 to 0.0625
- up_weight: bfloat16 [8192, 16384], P('width', 'blk'), may hold values from -0.0625 to 0.0625
- down_weight: bfloat16 [16384, 8192], P('blk', 'width'), may hold values from -0.046875 to 0.046875
- cotangent: bfloat16 [352, 8192], P(None, ('width', 'blk')), may hold values from -6 to 6
Outputs:
- output: bfloat16 [352, 8192], P(None, ('width', 'blk'))
- input_grad: bfloat16 [352, 8192], P(None, ('width', 'blk'))
- gate_weight_grad: float32 [8192, 16384], P('width', 'blk')
- up_weight_grad: float32 [8192, 16384], P('width', 'blk')
- down_weight_grad: float32 [16384, 8192], P('blk', 'width')
All inputs are finite; a program needn't handle non-finite values.
Results may differ from a plain program's by a relative error of at most 0.022.
Values may be sent and summed in bfloat16 or wider, within the bound.
A program may use at most 64 MiB of HBM per device.

v0:
```python
import jax
import jax.numpy as jnp
from jax import lax
from jax.sharding import PartitionSpec as P


def contract_rows(left, right):
    return lax.dot_general(
        left, right, (((0,), (0,)), ((), ())), preferred_element_type=jnp.float32
    )


def contract_cols(left, right):
    return lax.dot_general(
        left, right, (((1,), (1,)), ((), ())), preferred_element_type=jnp.float32
    )


def body(tokens, gate_weight, up_weight, down_weight, cotangent):
    gathered = lax.all_gather(tokens, "blk", axis=1, tiled=True)
    gate_part = jnp.dot(gathered, gate_weight, preferred_element_type=jnp.float32)
    up_part = jnp.dot(gathered, up_weight, preferred_element_type=jnp.float32)
    gate_pre, up_pre = lax.psum((gate_part, up_part), "width")
    sigmoid_gate = jax.nn.sigmoid(gate_pre)
    hidden = (gate_pre * sigmoid_gate * up_pre).astype(jnp.bfloat16)
    output_part = jnp.dot(hidden, down_weight, preferred_element_type=jnp.float32)
    output = lax.psum_scatter(output_part, "blk", scatter_dimension=1, tiled=True).astype(
        jnp.bfloat16
    )
    grads_all = lax.all_gather(cotangent, "blk", axis=1, tiled=True)
    down_weight_grad = contract_rows(hidden, grads_all)
    hidden_part = contract_cols(grads_all, down_weight)
    hidden_grad = lax.psum(hidden_part.astype(jnp.bfloat16), "width").astype(jnp.float32)
    gate_grad = (
        hidden_grad * up_pre * sigmoid_gate * (1.0 + gate_pre * (1.0 - sigmoid_gate))
    ).astype(jnp.bfloat16)
    up_grad = (hidden_grad * gate_pre * sigmoid_gate).astype(jnp.bfloat16)
    gate_weight_grad = contract_rows(gathered, gate_grad)
    up_weight_grad = contract_rows(gathered, up_grad)
    input_part = contract_cols(gate_grad, gate_weight) + contract_cols(up_grad, up_weight)
    input_grad = lax.psum_scatter(input_part, "blk", scatter_dimension=1, tiled=True).astype(
        jnp.bfloat16
    )
    return (output, input_grad, gate_weight_grad, up_weight_grad, down_weight_grad)


def solution(mesh):
    return jax.shard_map(
        body,
        mesh=mesh,
        in_specs=(
            P(None, ("width", "blk")),
            P("width", "blk"),
            P("width", "blk"),
            P("blk", "width"),
            P(None, ("width", "blk")),
        ),
        out_specs=(
            P(None, ("width", "blk")),
            P(None, ("width", "blk")),
            P("width", "blk"),
            P("width", "blk"),
            P("blk", "width"),
        ),
        check_vma=False,
    )
```

profile of v0, /device:TPU:6, one launch (start us, length us, event | category | flops | bytes accessed | tf_op | source)
XLA Modules:
  0.0 2188.6 jit_solution(15052067071563734931)
XLA Ops:
  7.2 0.0 copy-start
  7.2 0.0 copy-start.6
  7.2 0.0 copy-start.4
  7.2 0.0 all-reduce.4.cloned.1.call-start
  7.2 212.4 %all_gather.7 = bf16[352,1024]{0,1:T(8,128)(2,1)S(1)} all-gather(bf16[352,16]{0,1:T(8,128)(2,1)} %param.9), channel_id=1, replica_groups=mesh['blk'=64,'width'=8] {'blk'}, dimensions={1}, use_global_device_ids=true | all-gather | bytes 732160 | tf_op jit(solution)/shard_map/all_gather | solution.py:30
  219.6 0.0 copy-done
  219.6 1.1 convolution_convert_fusion
  220.7 0.0 copy-start.3
  220.7 0.0 all-reduce.4.cloned.1.call-update
  220.7 0.0 all-reduce.6.cloned.1.call-start
  220.8 0.0 copy-done.6
  220.8 198.4 %all_gather.6 = bf16[352,1024]{0,1:T(8,128)(2,1)S(1)} all-gather(bf16[352,16]{0,1:T(8,128)(2,1)S(1)} %copy-done.6), channel_id=1, replica_groups=mesh['blk'=64,'width'=8] {'blk'}, dimensions={1}, use_global_device_ids=true | all-gather | bytes 732160 | tf_op jit(solution)/shard_map/all_gather | solution.py:20
  419.2 0.0 copy-done.4
  419.2 1.1 fusion.8
  420.3 0.0 copy-done.3
  420.3 1.1 fusion.7
  421.5 0.0 all-reduce.6.cloned.1.call-update
  421.5 0.0 reduce-scatter.3.cloned.1.call-start
  421.5 0.0 all-reduce.4.cloned.1.call-done
  421.6 110.8 %all-reduce.6.cloned.1.call-done = (f32[352,256]{1,0:T(8,128)}, f32[352,256]{1,0:T(8,128)}) async-done(((f32[352,256]{1,0:T(8,128)}, f32[352,256]{1,0:T(8,128)}), (f32[352,256]{1,0:T(8,128)}, f32[352,256]{1,0:T(8,128)})) %all-reduce.6.cloned.1.call-update) | async-done | bytes 720912 | tf_op jit(solution)/shard_map/psum | solution.py:23
  532.4 1.4 fusion.2
  533.8 1.6 fusion.9
  535.4 0.0 copy-start.1
  535.4 0.0 copy-start.2
  535.4 0.0 reduce-scatter.3.cloned.1.call-update
  535.4 0.0 reduce-scatter.5.cloned.1.call-start
  535.5 0.0 copy-start.5
  535.5 0.5 fusion.10
  535.9 0.4 copy-done.1
  536.4 0.0 copy-done.2
  536.4 0.2 copy-done.5
  536.7 1.7 convolution_add_fusion
  538.3 0.0 reduce-scatter.5.cloned.1.call-update
  538.3 0.5 convolution_bitcast_fusion.1
  538.8 1.3 copy.10
  540.1 1.5 convolution_bitcast_fusion
  541.7 1.3 copy.11
  543.0 1.4 fusion.11
  544.4 814.4 %reduce-scatter.3.cloned.1.call-done = f32[352,16]{0,1:T(8,128)} async-done(((f32[352,1024]{0,1:T(8,128)}), f32[352,16]{0,1:T(8,128)}) %reduce-scatter.3.cloned.1.call-update) | async-done | bytes 22544 | tf_op jit(solution)/shard_map/reduce_scatter | solution.py:27
  1358.8 1.3 convert_element_type.22
  1360.2 820.6 %reduce-scatter.5.cloned.1.call-done = f32[352,16]{0,1:T(8,128)} async-done(((f32[352,1024]{0,1:T(8,128)}), f32[352,16]{0,1:T(8,128)}) %reduce-scatter.5.cloned.1.call-update) | async-done | bytes 22544 | tf_op jit(solution)/shard_map/reduce_scatter | solution.py:41
  2180.7 1.3 convert_element_type.27
Async XLA Ops:
  7.2 212.5 %copy-start = (bf16[256,1024]{1,0:T(8,128)(2,1)S(1)}, bf16[256,1024]{1,0:T(8,128)(2,1)}, u32[]{:S(2)}) copy-start(bf16[256,1024]{1,0:T(8,128)(2,1)} %param.8) | copy-start | bytes 1572868
  7.2 213.6 %copy-start.6 = (bf16[352,16]{0,1:T(8,128)(2,1)S(1)}, bf16[352,16]{0,1:T(8,128)(2,1)}, u32[]{:S(2)}) copy-start(bf16[352,16]{0,1:T(8,128)(2,1)} %param.5) | copy-start | bytes 33796
  7.2 412.0 %copy-start.4 = (bf16[1024,256]{1,0:T(8,128)(2,1)S(1)}, bf16[1024,256]{1,0:T(8,128)(2,1)}, u32[]{:S(2)}) copy-start(bf16[1024,256]{1,0:T(8,128)(2,1)} %param.7) | copy-start | bytes 1572868
  7.2 414.4 %all-reduce.4.cloned.1.call-start = ((), (), s32[]{:S(2)}) async-start(), calls=%async_computation.3 | async-start | bytes 360448 | tf_op jit(solution)/shard_map/psum | solution.py:33
  220.7 199.6 %copy-start.3 = (bf16[1024,256]{1,0:T(8,128)(2,1)S(1)}, bf16[1024,256]{1,0:T(8,128)(2,1)}, u32[]{:S(2)}) copy-start(bf16[1024,256]{1,0:T(8,128)(2,1)} %param.6) | copy-start | bytes 1572868
  220.7 311.6 %all-reduce.6.cloned.1.call-start = ((), (), s32[]{:S(2)}) async-start(), calls=%async_computation.5 | async-start | bytes 1441792 | tf_op jit(solution)/shard_map/psum | solution.py:23
  421.5 937.3 %reduce-scatter.3.cloned.1.call-start = ((), (), s32[]{:S(2)}) async-start(), calls=%async_computation.2 | async-start | bytes 1597440 | tf_op jit(solution)/shard_map/reduce_scatter | solution.py:27
  535.4 1.0 copy-start.1
  535.4 1.0 copy-start.2
  535.4 1645.3 %reduce-scatter.5.cloned.1.call-start = ((), (), s32[]{:S(2)}) async-start(), calls=%async_computation.4 | async-start | bytes 1597440 | tf_op jit(solution)/shard_map/reduce_scatter | solution.py:41
  535.5 1.2 copy-start.5
Sparse Core Ops, SparseCore 0:
  220.9 88.5 all-reduce.3
  421.6 110.7 all-reduce.5
  539.9 818.8 reduce-scatter.2
  1365.1 815.6 reduce-scatter.4
where the time goes:
time: 2190 us
  waiting for transfers between devices  1750 us (80%)
  blocking collectives  411 us (19%)
    reduce_scatter x1, waiting for transfers between devices, body(): lax.psum_scatter(input_part, 'blk', scatter_dimension=1, tiled=True)  821 us
    reduce_scatter x1, waiting for transfers between devices, body(): lax.psum_scatter(output_part, 'blk', scatter_dimension=1, tiled=True)  814 us
    all_gather x1, blocking collectives, body(): grads_all = lax.all_gather(cotangent, 'blk', axis=1, tiled=True)  212 us
    all_gather x1, blocking collectives, body(): gathered = lax.all_gather(tokens, 'blk', axis=1, tiled=True)  198 us
    psum x1, waiting for transfers between devices, body(): gate_pre, up_pre = lax.psum((gate_part, up_part), 'width')  111 us
  transfers between devices with their start and end apart: 4, of which 3 were waited for; matrix products, arithmetic and copies ran while one was open for 1% of the time, Pallas kernels for 0%

commit v1 on v0

v1 whole, which is shorter than its diff:
```python
import functools

import jax
import jax.numpy as jnp
from jax import lax
from jax.experimental import pallas as pl
from jax.experimental.pallas import tpu as pltpu
from jax.sharding import PartitionSpec as P

MESH = pl.DeviceIdType.MESH
X, ZH, Y = 4, 2, 8
ZL, CORES = 4, 2
F32, BF16 = jnp.float32, jnp.bfloat16


def mm(left, right, dims):
    return lax.dot_general(left, right, ((dims[:1], dims[1:]), ((), ())), preferred_element_type=F32)


class Sems:
    def __init__(self, send, recv):
        self.send, self.recv, self.used, self.live = send, recv, 0, []

    def copy(self, src, dst, device):
        i = self.used
        self.used += 1
        c = pltpu.make_async_remote_copy(
            src_ref=src, dst_ref=dst, send_sem=self.send.at[i], recv_sem=self.recv.at[i],
            device_id=device, device_id_type=MESH,
        )
        c.start()
        self.live.append(c)
        return c


def turns(*gens):
    gens = list(gens)
    while gens:
        for g in list(gens):
            try:
                next(g)
            except StopIteration:
                gens.remove(g)


def kernel(
    tok_ref, cot_ref, gw_hbm, uw_hbm, dw_hbm,
    out_ref, inp_ref, gwg_hbm, uwg_hbm, dwg_hbm,
    gw, uw, dw, gwg, uwg, dwg, G, PF, P16, C1, SZ, RZ, H, OT, SA, RA, SX, RX, ACC, SF, RF, SD, RD, SY, RY, SW, RW,
    send_sem, recv_sem, local_sem,
):
    b, w = lax.axis_index("blk"), lax.axis_index("width")
    x, zh, y = b // (ZH * Y), (b // Y) % ZH, b % Y
    zl, core = w // CORES, w % CORES
    oz, oc = 1 - zh, 1 - core
    tokens = tok_ref.shape[0]
    T = G.shape[-1]

    def xs(d):
        return (x + d) % X

    def ys(d):
        return (y + d) % Y

    def at_xy(d_x, d_y):
        return ((xs(d_x) * ZH + zh) * Y + ys(d_y), w)

    xdev = {d: at_xy(d, 0) for d in range(1, X)}
    ydev = {1: at_xy(0, 1), -1: at_xy(0, Y - 1)}
    xdev[-1] = xdev[X - 1]
    zdev = ((x * ZH + oz) * Y + y, w)
    cdev = (b, zl * CORES + oc)
    ldev = {d: (b, ((zl + d) % ZL) * CORES + core) for d in range(1, ZL)}

    loads = [
        pltpu.make_async_copy(s, d, local_sem.at[i])
        for i, (s, d) in enumerate(((gw_hbm, gw), (uw_hbm, uw), (dw_hbm, dw)))
    ]
    for c in loads:
        c.start()

    barrier = pltpu.get_barrier_semaphore()
    partners = [xdev[d] for d in range(1, X)] + [ydev[1], ydev[-1], zdev, cdev] + [ldev[d] for d in range(1, ZL)]
    for p in partners:
        pl.semaphore_signal(barrier, inc=1, device_id=p, device_id_type=MESH)

    eye = (
        lax.broadcasted_iota(jnp.int32, (16, 16), 0) == lax.broadcasted_iota(jnp.int32, (16, 16), 1)
    ).astype(F32).astype(BF16)
    for t, ref in enumerate((tok_ref, cot_ref)):
        G[t, x, zh, y] = mm(eye, jnp.pad(ref[...], ((0, T - tokens), (0, 0))), (1, 1)).astype(BF16)
    pl.semaphore_wait(barrier, len(partners))

    sems = Sems(send_sem, recv_sem)

    def gather_a(t):
        own = G.at[t, x, zh, y]
        xm = {d: sems.copy(own, own, xdev[d]) for d in range(1, X)}
        yield
        R, L = {}, {}
        far = {d: (4, 3) if d % 2 == 0 else (3, 4) for d in range(X)}
        for k in range(5):
            for d in range(X):
                if k == 0 and d > 0:
                    xm[d].wait_recv()
                for M, sign, n in ((R, 1, far[d][0]), (L, -1, far[d][1])):
                    if 0 < k <= n:
                        M[k - 1, d].wait_recv()
                    if k < n:
                        piece = G.at[t, xs(X - d), zh, ys(Y - sign * k)]
                        M[k, d] = sems.copy(piece, piece, ydev[sign])
                yield

    def gather_b(t, zm):
        zm.wait_recv()
        R, L, XR, XL, XF = {}, {}, {}, {}, {}
        done = []

        def spread(k):
            yk = ys(Y - k)
            piece = G.at[t, x, oz, yk]
            XR[k] = sems.copy(piece, piece, xdev[1])
            XL[k] = sems.copy(piece, piece, xdev[-1])
            done.append(k)

        def forward(k):
            yk = ys(Y - k)
            if k % 2 == 0:
                XR[k].wait_recv()
                piece = G.at[t, xs(X - 1), oz, yk]
                XF[k] = sems.copy(piece, piece, xdev[1])
            else:
                XL[k].wait_recv()
                piece = G.at[t, xs(1), oz, yk]
                XF[k] = sems.copy(piece, piece, xdev[-1])

        for k in range(5):
            for M, sign, n in ((R, 1, 4), (L, -1, 3)):
                if 0 < k <= n:
                    M[k - 1].wait_recv()
                if k < n:
                    piece = G.at[t, x, oz, ys(Y - sign * k)]
                    M[k] = sems.copy(piece, piece, ydev[sign])
            old = list(done)
            for sign, n in ((1, 4), (-1, 3)):
                if k <= n and (k > 0 or sign > 0):
                    spread(sign * k)
            yield
            for j in old:
                if j not in XF:
                    forward(j)
            yield
        for j in done:
            if j not in XF:
                forward(j)
        yield
        for j in done:
            (XL if j % 2 == 0 else XR)[j].wait_recv()
            XF[j].wait_recv()

    def width_sum(a0, na, result):
        a = pl.ds(a0, na)
        P16[a] = PF[a, oc].astype(BF16)
        cm = sems.copy(P16.at[a], C1.at[a], cdev)
        yield
        cm.wait_recv()
        zm = {}
        for d in (2, 1, 3):
            j = (zl + d) % ZL
            SZ[d, a] = (PF[a, core, j] + C1[a, j].astype(F32)).astype(BF16)
            zm[d] = sems.copy(SZ.at[d, a], RZ.at[d, a], ldev[d])
        total = PF[a, core, zl] + C1[a, zl].astype(F32)
        yield
        for d in (1, 3, 2):
            zm[d].wait_recv()
            total = total + RZ[d, a].astype(F32)
        PF[a, core, zl] = total
        result()

    def width_gather(a0, na):
        a = pl.ds(a0, na)
        own = H.at[a, core, zl]
        zm = {d: sems.copy(own, own, ldev[d]) for d in (2, 1, 3)}
        cm = {0: sems.copy(own, own, cdev)}
        yield
        for d in (1, 3, 2):
            zm[d].wait_recv()
            piece = H.at[a, core, (zl + ZL - d) % ZL]
            cm[d] = sems.copy(piece, piece, cdev)
            yield
        for d in (0, 1, 3, 2):
            cm[d].wait_recv()

    def make_hidden():
        g, u = PF[0, core, zl], PF[1, core, zl]
        s = 1.0 / (1.0 + jnp.exp(-g))
        H[0, core, zl] = (g * s * u).astype(BF16)

    def make_grads():
        g, u, h = PF[0, core, zl], PF[1, core, zl], PF[2, core, zl]
        s = 1.0 / (1.0 + jnp.exp(-g))
        H[1, core, zl] = (h * u * s * (1.0 + g * (1.0 - s))).astype(BF16)
        H[2, core, zl] = (h * g * s).astype(BF16)

    def scatter_a(t):
        R, L, xm = {}, {}, {}
        far = {d: (4, 3) if d % 2 == 0 else (3, 4) for d in range(X)}
        order = (1, 2, 3, 0)
        for k in range(5):
            for d in order:
                for M, i, sign, n in ((R, 0, 1, far[d][0]), (L, 1, -1, far[d][1])):
                    if 0 < k <= n:
                        M[k - 1, d].wait_recv()
                    if k < n:
                        v = OT[t, xs(d), zh, ys(Y + sign * (n - k))]
                        if k > 0:
                            v = v + RA[t, i, k - 1, d].astype(F32)
                        SA[t, i, k, d] = v.astype(BF16)
                        M[k, d] = sems.copy(SA.at[t, i, k, d], RA.at[t, i, k, d], ydev[sign])
                if k == 4:
                    v = OT[t, xs(d), zh, y]
                    v = v + RA[t, 0, far[d][0] - 1, d].astype(F32) + RA[t, 1, far[d][1] - 1, d].astype(F32)
                    if d > 0:
                        SX[t, d] = v.astype(BF16)
                        xm[d] = sems.copy(SX.at[t, d], RX.at[t, d], xdev[d])
                    else:
                        ACC[t] = v
                yield
        for d in order[:-1]:
            xm[d].wait_recv()
            ACC[t] += RX[t, d].astype(F32)

    def scatter_b(t):
        order = (4, 5, 3, 6, 2, 7, 1, 0)
        F, D = {}, {}
        for j in order:
            SF[t, j] = OT[t, xs(2), oz, ys(j)].astype(BF16)
            F[j] = sems.copy(SF.at[t, j], RF.at[t, j], xdev[1 if j % 2 == 0 else -1])
        yield
        for j in order:
            for i, sign in ((0, 1), (1, -1)):
                if (j % 2 == 0) != (sign > 0):
                    SD[t, i, j] = OT[t, xs(sign % X), oz, ys(j)].astype(BF16)
                    D[i, j] = sems.copy(SD.at[t, i, j], RD.at[t, i, j], xdev[sign])
        yield
        for n, j in enumerate(order):
            i, sign = (0, 1) if j % 2 == 0 else (1, -1)
            F[j].wait_recv()
            SD[t, i, j] = (OT[t, xs(sign % X), oz, ys(j)] + RF[t, j].astype(F32)).astype(BF16)
            D[i, j] = sems.copy(SD.at[t, i, j], RD.at[t, i, j], xdev[sign])
            if n % 2:
                yield

        def take(j):
            D[0, j].wait_recv()
            D[1, j].wait_recv()
            return OT[t, x, oz, ys(j)] + RD[t, 0, j].astype(F32) + RD[t, 1, j].astype(F32)

        R, L = {}, {}
        for k in range(4):
            for M, i, sign, n in ((R, 0, 1, 4), (L, 1, -1, 3)):
                if k < n:
                    v = take(sign * (n - k) % Y)
                    if k > 0:
                        M[k - 1].wait_recv()
                        v = v + RY[t, i, k - 1].astype(F32)
                    SY[t, i, k] = v.astype(BF16)
                    M[k] = sems.copy(SY.at[t, i, k], RY.at[t, i, k], ydev[sign])
            yield
        v = take(0)
        L[2].wait_recv()
        v = v + RY[t, 1, 2].astype(F32)
        R[3].wait_recv()
        v = v + RY[t, 0, 3].astype(F32)
        SW[t] = v.astype(BF16)
        wm = sems.copy(SW.at[t], RW.at[t], zdev)
        yield
        wm.wait_recv()

    def finish(t, ref):
        v = (ACC[t] + RW[t].astype(F32)).astype(BF16)
        ref[...] = mm(v, eye, (0, 0))[:tokens].astype(BF16)

    def hid(i):
        return H[i].reshape(dw.shape[0], T)

    def rows(t, i):
        return G[t, i].reshape(ZH * Y * 16, T)

    span = ZH * Y * 16

    def put(t, i, v):
        OT[t, i] = v.reshape(ZH, Y, 16, T)

    def grads(t):
        for i in range(X):
            s = pl.ds(i * span, span)
            if t == 0:
                dwg[:, s] = mm(hid(0), rows(1, i), (1, 1))
                yield
            else:
                gwg[s, :] = mm(rows(0, i), hid(1), (1, 1))
                yield
                uwg[s, :] = mm(rows(0, i), hid(2), (1, 1))
                yield

    zm = [None, None]
    for t in range(2):
        own = G.at[t, x, zh, y]
        zm[t] = sems.copy(own, own, zdev)
    tok = [gather_a(0), gather_b(0, zm[0])]
    turns(*tok)
    cot = [gather_a(1), gather_b(1, zm[1])]
    for g in cot:
        next(g)
    full = (CORES, ZL, -1, T)
    loads[0].wait()
    loads[1].wait()
    PF[0] = mm(gw[...], G[0].reshape(-1, T), (0, 0)).reshape(PF.shape[1:])
    PF[1] = mm(uw[...], G[0].reshape(-1, T), (0, 0)).reshape(PF.shape[1:])

    def early():
        yield from width_sum(0, 2, make_hidden)
        yield from width_gather(0, 1)

    turns(*cot, early())
    loads[2].wait()
    PF[2] = mm(dw[...], G[1].reshape(-1, T), (1, 0)).reshape(PF.shape[1:])
    late = width_sum(2, 1, make_grads)
    next(late)
    for i in range(X):
        put(0, i, mm(dw[:, i * span : (i + 1) * span], hid(0), (0, 0)))

    def mid():
        yield from late
        yield from width_gather(1, 2)

    out = [scatter_a(0), scatter_b(0)]
    turns(mid(), *out, grads(0))
    stores = [pltpu.make_async_copy(dwg, dwg_hbm, local_sem.at[3])]
    stores[0].start()
    for i in range(X):
        s = pl.ds(i * span, span)
        put(1, i, mm(gw[s, :], hid(1), (1, 0)) + mm(uw[s, :], hid(2), (1, 0)))
    turns(scatter_a(1), scatter_b(1), grads(1))
    stores.append(pltpu.make_async_copy(gwg, gwg_hbm, local_sem.at[4]))
    stores.append(pltpu.make_async_copy(uwg, uwg_hbm, local_sem.at[5]))
    stores[1].start()
    stores[2].start()
    finish(0, out_ref)
    finish(1, inp_ref)
    for c in sems.live:
        c.wait_send()
    for c in stores:
        c.wait()
    assert sems.used <= send_sem.shape[0], sems.used


def body(tokens, gate_weight, up_weight, down_weight, cotangent):
    n, (depth, hidden) = tokens.shape[0], gate_weight.shape
    T = -(-n // 128) * 128
    V = pltpu.VMEM
    part = hidden // (CORES * ZL)
    scratch = [
        V(gate_weight.shape, BF16), V(up_weight.shape, BF16), V(down_weight.shape, BF16),
        V(gate_weight.shape, F32), V(up_weight.shape, F32), V(down_weight.shape, F32),
        V((2, X, ZH, Y, 16, T), BF16),
        V((3, CORES, ZL, part, T), F32),
        V((3, ZL, part, T), BF16), V((3, ZL, part, T), BF16),
        V((ZL, 3, part, T), BF16), V((ZL, 3, part, T), BF16),
        V((3, CORES, ZL, part, T), BF16),
        V((2, X, ZH, Y, 16, T), F32),
        V((2, 2, 4, X, 16, T), BF16), V((2, 2, 4, X, 16, T), BF16),
        V((2, X, 16, T), BF16), V((2, X, 16, T), BF16),
        V((2, 16, T), F32),
        V((2, Y, 16, T), BF16), V((2, Y, 16, T), BF16),
        V((2, 2, Y, 16, T), BF16), V((2, 2, Y, 16, T), BF16),
        V((2, 2, 4, 16, T), BF16), V((2, 2, 4, 16, T), BF16),
        V((2, 16, T), BF16), V((2, 16, T), BF16),
        pltpu.SemaphoreType.DMA((300,)),
        pltpu.SemaphoreType.DMA((300,)),
        pltpu.SemaphoreType.DMA((6,)),
    ]
    vm, anywhere = pl.BlockSpec(memory_space=V), pl.BlockSpec(memory_space=pl.ANY)
    S = jax.ShapeDtypeStruct
    return pl.pallas_call(
        kernel,
        out_shape=(
            S(tokens.shape, BF16), S(tokens.shape, BF16),
            S(gate_weight.shape, F32), S(up_weight.shape, F32), S(down_weight.shape, F32),
        ),
        in_specs=[vm, vm, anywhere, anywhere, anywhere],
        out_specs=(vm, vm, anywhere, anywhere, anywhere),
        scratch_shapes=scratch,
        compiler_params=pltpu.CompilerParams(
            collective_id=0, has_side_effects=True, vmem_limit_bytes=48 * 2**20
        ),
        cost_estimate=pl.CostEstimate(flops=18 * n * depth * hidden, bytes_accessed=18 * depth * hidden, transcendentals=0),
        name="ffn",
    )(tokens, cotangent, gate_weight, up_weight, down_weight)


def solution(mesh):
    return jax.shard_map(
        body,
        mesh=mesh,
        in_specs=(
            P(None, ("width", "blk")),
            P("width", "blk"),
            P("width", "blk"),
            P("blk", "width"),
            P(None, ("width", "blk")),
        ),
        out_specs=(
            P(None, ("width", "blk")),
            P(None, ("width", "blk")),
            P("width", "blk"),
            P("width", "blk"),
            P("blk", "width"),
        ),
        check_vma=False,
    )
```

time: 2190 us -> 152 us (0.07)
  waiting for transfers between devices: 1750 us -> 0 us
  blocking collectives: 411 us -> 0 us
  Pallas kernels: 0 us -> 142 us
    reduce_scatter x2 -> x0, waiting for transfers between devices: 1630 us -> none  [the longest x1 821 us: body(): lax.psum_scatter(input_part, 'blk', scatter_dimension=1, tiled=True)]
    all_gather x2 -> x0, blocking collectives: 411 us -> none  [the longest x1 212 us: body(): grads_all = lax.all_gather(cotangent, 'blk', axis=1, tiled=True)]
    pallas_call x0 -> x1, Pallas kernels: none -> 142 us  [body(): pl.pallas_call(kernel, out_shape=(S(tokens.shape, BF16), S(tokens.shape,...]
    psum x2 -> x0, waiting for transfers between devices: 111 us -> none  [the longest x1 111 us: body(): gate_pre, up_pre = lax.psum((gate_part, up_part), 'width')]
  transfers between devices with their start and end apart: 4 -> 0, of which waited for: 3 -> 0; matrix products, arithmetic and copies ran while one was open for 1% -> 0% of each run, Pallas kernels for 0% -> 0%
where the time goes in v1:
time: 152 us; the launch traced here: 151 us
  Pallas kernels  142 us (93%)
  local copies, waits for them, and re-layouts  8.36 us (6%)
    pallas_call x1, Pallas kernels, body(): pl.pallas_call(kernel, out_shape=(S(tokens.shape, BF16), S(tokens.shape,...  142 us
    unnamed x13, local copies, waits for them, and re-layouts  6.99 us

profile of v1, /device:TPU:6, one launch (start us, length us, event | category | flops | bytes accessed | tf_op | source)
XLA Modules:
  0.0 151.2 jit_solution(12556915129142594807)
XLA Ops:
  0.6 0.0 copy-start.3
  0.6 0.8 copy.10.tok_ref
  1.5 0.0 copy-done.3
  1.5 0.1 copy.11.cot_ref
  1.6 0.0 copy-start
  1.6 1.0 copy-done
  2.7 0.0 copy-start.1
  2.7 1.0 copy-done.1
  3.7 0.0 copy-start.2
  3.7 1.0 copy-done.2
  4.7 142.2 %ffn.1 = (bf16[352,16]{1,0:T(8,128)(2,1)S(1)}, bf16[352,16]{1,0:T(8,128)(2,1)S(1)}, f32[1024,256]{1,0:T(8,128)S(1)}, f32[1024,256]{1,0:T(8,128)S(1)}, f32[256,1024]{1,0:T(8,128)S(1)}) custom-call(bf16[352,16]{1,0:T(8,128)(2,1)S(1)} %copy.10.tok_ref, bf16[352,16]{1,0:T(8,128)(2,1)S(1)} %copy.11.cot_ref, bf16[1024,256]{1,0:T(8,128)(2,1)S(1)} %copy-done, ...), custom_call_target="tpu_custom_call" | custom-call | flops 1660944384 | bytes 4718592 | tf_op jit(solution)/shard_map/ffn/pallas_call | solution.py:386
  147.0 0.7 copy.12
  147.7 0.7 copy.13
  148.3 1.0 copy.17
  149.3 1.0 copy.18
  150.3 1.0 copy.19
Async XLA Ops:
  0.6 0.8 copy-start.3
  1.6 1.0 copy-start
  2.7 1.0 copy-start.1
  3.7 1.0 copy-start.2

commit v2 on v0

v2 whole, which is shorter than its diff:
```python
import functools

import jax
import jax.numpy as jnp
from jax import lax
from jax.experimental import pallas as pl
from jax.experimental.pallas import tpu as pltpu
from jax.sharding import PartitionSpec as P

MESH = pl.DeviceIdType.MESH
X, ZH, Y = 4, 2, 8
ZL, CORES = 4, 2
F32, BF16 = jnp.float32, jnp.bfloat16


def mm(left, right, dims):
    return lax.dot_general(left, right, ((dims[:1], dims[1:]), ((), ())), preferred_element_type=F32)


class Sems:
    def __init__(self, send, recv):
        self.send, self.recv, self.used, self.live = send, recv, 0, []

    def copy(self, src, dst, device):
        i = self.used
        self.used += 1
        c = pltpu.make_async_remote_copy(
            src_ref=src, dst_ref=dst, send_sem=self.send.at[i], recv_sem=self.recv.at[i],
            device_id=device, device_id_type=MESH,
        )
        c.start()
        self.live.append(c)
        return c


def turns(*gens):
    gens = list(gens)
    while gens:
        for g in list(gens):
            try:
                next(g)
            except StopIteration:
                gens.remove(g)


def kernel(
    tok_hbm, cot_hbm, gw_hbm, uw_hbm, dw_hbm,
    out_hbm, inp_hbm, gwg_hbm, uwg_hbm, dwg_hbm,
    io, gw, uw, dw, gwT, uwT, dwT, gwg, uwg, dwg, G, PF, P16, C1, SZ, RZ, H, OT,
    SA, RA, SF, RF, SX, RX, ACC, SD, RD, SY, RY, SW, RW,
    send_sem, recv_sem, local_sem,
):
    b, w = lax.axis_index("blk"), lax.axis_index("width")
    x, zh, y = b // (ZH * Y), (b // Y) % ZH, b % Y
    zl, core = w // CORES, w % CORES
    oz, oc = 1 - zh, 1 - core
    tokens = io.shape[-1]
    T = G.shape[-1]
    span = ZH * Y * 16

    def xs(d):
        return (x + d % X) % X

    def ys(d):
        return (y + d % Y) % Y

    xdev = {d: ((xs(d) * ZH + zh) * Y + y, w) for d in range(1, X)}
    ydev = {d: ((x * ZH + zh) * Y + ys(d), w) for d in (1, -1, 2, -2, 3, -3, 4)}
    zdev = ((x * ZH + oz) * Y + y, w)
    cdev = (b, zl * CORES + oc)
    ldev = {d: (b, ((zl + d) % ZL) * CORES + core) for d in range(1, ZL)}

    barrier = pltpu.get_barrier_semaphore()
    partners = [zdev] + list(ldev.values()) + list(ydev.values()) + list(xdev.values()) + [cdev]
    for p in partners:
        pl.semaphore_signal(barrier, inc=1, device_id=p, device_id_type=MESH)

    loads = [
        pltpu.make_async_copy(s, d, local_sem.at[i])
        for i, (s, d) in enumerate(
            ((tok_hbm, io.at[0]), (cot_hbm, io.at[1]), (gw_hbm, gw), (uw_hbm, uw), (dw_hbm, dw))
        )
    ]
    for c in loads:
        c.start()
    for t in range(2):
        loads[t].wait()
        G[t, 0, zh, y] = jnp.pad(io[t].astype(F32), ((0, 0), (0, T - tokens))).astype(BF16)
    for c in loads[2:]:
        c.wait()
    for i in range(X):
        s = slice(i * span, (i + 1) * span)
        gwT[i] = gw[s, :].T
        uwT[i] = uw[s, :].T
        dwT[i] = dw[:, s].T
    pl.semaphore_wait(barrier, len(partners))

    sems = Sems(send_sem, recv_sem)

    def cols(i):
        return pl.ds(pl.multiple_of(i * span, span), span)

    def block(t, d):
        return G[t, d].reshape(span, T)

    def part(t, d):
        i = xs(-d)
        v = block(t, d)
        if t == 0:
            new = (mm(gwT[i], v, (1, 0)), mm(uwT[i], v, (1, 0)))
        else:
            new = (mm(dw[:, cols(i)], v, (1, 0)),)
        for n, p in enumerate(new):
            p = p.reshape(PF.shape[1:])
            PF[2 * t + n] = p if d == 0 else PF[2 * t + n] + p

    def gather(t, zm):
        own, rest = G.at[t, 0, zh, y], G.at[t, pl.ds(1, X - 1), zh, y]
        near = (1, -1, 2, -2)
        xm = {d: sems.copy(own, G.at[t, d, zh, y], xdev[d]) for d in (2, 1, 3)}
        N1 = {e: sems.copy(own, own, ydev[e]) for e in near}
        yield
        for d in (1, 3, 2):
            xm[d].wait_recv()
        N2 = {e: sems.copy(rest, rest, ydev[e]) for e in (2, -2, 1, -1)}
        yield
        if t == 0:
            zm.wait_recv()
        other = G.at[t, 0, oz, y]
        B = {e: sems.copy(other, other, ydev[e]) for e in (1, -1, 2, -2, 3, -3, 4)}
        XB = {}

        def spread(e):
            piece = G.at[t, 0, oz, ys(-e)]
            for d in (2, 1, 3):
                XB[e, d] = sems.copy(piece, G.at[t, d, oz, ys(-e)], xdev[d])

        spread(0)
        yield
        F = []
        for s, half in ((1, pl.ds(0, X // 2)), (-1, pl.ds(X // 2, X // 2))):
            N1[2 * s].wait_recv()
            N2[2 * s].wait_recv()
            piece = G.at[t, half, zh, ys(-2 * s)]
            F.append(sems.copy(piece, piece, ydev[2 * s]))
            piece = G.at[t, :, zh, ys(-2 * s)]
            F.append(sems.copy(piece, piece, ydev[s]))
        yield
        for e in (1, -1, 2, -2, 3, -3, 4):
            B[e].wait_recv()
            spread(e)
            if e != 1 and e != 2 and e != 3:
                yield
        for e in (1, -1):
            N1[e].wait_recv()
            N2[e].wait_recv()
        for c in F:
            c.wait_recv()
        part(t, 0)
        yield
        for d in (1, 3, 2):
            for e in (0, 1, -1, 2, -2, 3, -3, 4):
                XB[e, d].wait_recv()
            part(t, d)

    def width_sum(a0, na, result):
        a = pl.ds(a0, na)
        P16[a] = PF[a, oc].astype(BF16)
        cm = sems.copy(P16.at[a], C1.at[a], cdev)
        yield
        cm.wait_recv()
        zm = {}
        for d in (3, 2, 1):
            j = (zl + d) % ZL
            SZ[d, a] = (PF[a, core, j] + C1[a, j].astype(F32)).astype(BF16)
            zm[d] = sems.copy(SZ.at[d, a], RZ.at[d, a], ldev[d])
        total = PF[a, core, zl] + C1[a, zl].astype(F32)
        PF[a, core, zl] = total
        yield
        for d in (1, 3, 2):
            zm[d].wait_recv()
            total = total + RZ[d, a].astype(F32)
        PF[a, core, zl] = total
        result()

    def width_gather(a0, na):
        a = pl.ds(a0, na)
        own = H.at[a, core, zl]
        zm = {d: sems.copy(own, own, ldev[d]) for d in (3, 2, 1)}
        cm = {0: sems.copy(own, own, cdev)}
        yield
        for d in (1, 3, 2):
            zm[d].wait_recv()
            piece = H.at[a, core, (zl + ZL - d) % ZL]
            cm[d] = sems.copy(piece, piece, cdev)
        yield
        for d in (0, 1, 3, 2):
            cm[d].wait_recv()

    def make_hidden():
        g, u = PF[0, core, zl], PF[1, core, zl]
        s = 1.0 / (1.0 + jnp.exp(-g))
        H[0, core, zl] = (g * s * u).astype(BF16)

    def make_grads():
        g, u, h = PF[0, core, zl], PF[1, core, zl], PF[2, core, zl]
        s = 1.0 / (1.0 + jnp.exp(-g))
        H[1, core, zl] = (h * u * s * (1.0 + g * (1.0 - s))).astype(BF16)
        H[2, core, zl] = (h * g * s).astype(BF16)

    def scatter_a(t):
        halves = {1: pl.ds(0, X // 2), -1: pl.ds(X // 2, X // 2)}
        F4, M = {}, {}

        def send(i, v, device):
            SA[t, i] = v.astype(BF16)
            M[i] = sems.copy(SA.at[t, i], RA.at[t, i], device)

        for i, s in enumerate((1, -1)):
            SF[t, i] = OT[t, halves[s], zh, ys(4)].astype(BF16)
            F4[i] = sems.copy(SF.at[t, i], RF.at[t, i], ydev[2 * s])
            send(i, OT[t, :, zh, ys(3 * s)], ydev[s])
        yield
        for i, s in enumerate((1, -1)):
            send(2 + i, OT[t, :, zh, ys(s)], ydev[s])
        yield
        for i, s in enumerate((1, -1)):
            M[i].wait_recv()
            F4[i].wait_recv()
            OT[t, halves[s], zh, ys(2 * s)] += RF[t, i].astype(F32)
            send(4 + i, OT[t, :, zh, ys(2 * s)] + RA[t, i].astype(F32), ydev[2 * s])
        yield
        v = OT[t, :, zh, y]
        for i in (2, 3, 4, 5):
            M[i].wait_recv()
            v = v + RA[t, i].astype(F32)
        SX[t] = v[1:].astype(BF16)
        xm = {d: sems.copy(SX.at[t, d - 1], RX.at[t, d - 1], xdev[d]) for d in (2, 1, 3)}
        ACC[t] = v[0]
        yield
        for d in (1, 3, 2):
            xm[d].wait_recv()
            ACC[t] += RX[t, d - 1].astype(F32)

    def scatter_b(t):
        order = (4, -3, 3, -2, 2, -1, 1, 0)
        groups = ((0, 3), (3, 5), (5, 8))
        D, M = {}, {}
        for lo, hi in groups:
            for n in range(lo, hi):
                SD[t, :, n] = OT[t, pl.ds(1, X - 1), oz, ys(order[n])].astype(BF16)
            for d in (2, 1, 3):
                at = (t, d - 1, pl.ds(lo, hi - lo))
                D[lo, d] = sems.copy(SD.at[at], RD.at[at], xdev[d])
        yield
        for lo, hi in groups:
            for d in (1, 3, 2):
                D[lo, d].wait_recv()
            for n in range(lo, hi):
                v = OT[t, 0, oz, ys(order[n])]
                for d in range(1, X):
                    v = v + RD[t, d - 1, n].astype(F32)
                if order[n]:
                    SY[t, n] = v.astype(BF16)
                    M[n] = sems.copy(SY.at[t, n], RY.at[t, n], ydev[order[n]])
            yield
        for n in (5, 6, 3, 4, 1, 2, 0):
            M[n].wait_recv()
            v = v + RY[t, n].astype(F32)
        SW[t] = v.astype(BF16)
        M[7] = sems.copy(SW.at[t], RW.at[t], zdev)
        yield
        M[7].wait_recv()

    def hid(i):
        return H[i].reshape(dw.shape[0], T)

    def grads():
        for d in range(X):
            i = xs(-d)
            dwg[:, cols(i)] = mm(hid(0), block(1, d), (1, 1))
            yield
            gwg[cols(i), :] = mm(block(0, d), hid(1), (1, 1))
            yield
            uwg[cols(i), :] = mm(block(0, d), hid(2), (1, 1))
            yield

    def put(t, d, v):
        OT[t, d] = v.reshape(ZH, Y, 16, T)

    def drain(g):
        for _ in g:
            pass

    both = G.at[:, 0, zh, y]
    zm = sems.copy(both, both, zdev)
    tok, cot = gather(0, zm), gather(1, zm)
    left = True
    while left:
        left = False
        for _ in tok:
            left = True
            break
        if left:
            next(cot)
    pre = width_sum(0, 2, make_hidden)
    next(pre)
    next(pre)
    drain(cot)
    post = width_sum(2, 1, make_grads)
    next(post)
    next(post)
    drain(pre)
    fore = width_gather(0, 1)
    next(fore)
    drain(post)
    back = width_gather(1, 2)
    next(back)
    drain(fore)
    for d in range(X):
        put(0, d, mm(dwT[xs(d)], hid(0), (1, 0)))
    out = [scatter_b(0), scatter_a(0)]
    for g in out:
        next(g)
    drain(back)
    for d in range(X):
        i = xs(d)
        put(1, d, mm(gw[cols(i), :], hid(1), (1, 0)) + mm(uw[cols(i), :], hid(2), (1, 0)))
    turns(scatter_b(1), scatter_a(1), *out, grads())
    stores = []

    def store(src, dst):
        c = pltpu.make_async_copy(src, dst, local_sem.at[5 + len(stores)])
        c.start()
        stores.append(c)

    for src, dst in ((dwg, dwg_hbm), (gwg, gwg_hbm), (uwg, uwg_hbm)):
        store(src, dst)
    for t, ref in enumerate((out_hbm, inp_hbm)):
        io[t] = (ACC[t] + RW[t].astype(F32)).astype(BF16)[:, :tokens]
        store(io.at[t], ref)
    for c in sems.live:
        c.wait_send()
    for c in stores:
        c.wait()
    assert sems.used <= send_sem.shape[0], sems.used


def hand_on(*refs):
    n = len(refs) // 2
    copies = [pltpu.make_async_copy(refs[i], refs[n + i], refs[-1].at[i]) for i in range(n)]
    for c in copies:
        c.start()
    for c in copies:
        c.wait()


def body(tokens, gate_weight, up_weight, down_weight, cotangent):
    n, (depth, hidden) = tokens.shape[0], gate_weight.shape
    T = -(-n // 128) * 128
    V = pltpu.VMEM
    part, span = hidden // (CORES * ZL), ZH * Y * 16
    scratch = [
        V((2, 16, n), BF16),
        V(gate_weight.shape, BF16), V(up_weight.shape, BF16), V(down_weight.shape, BF16),
        V((X, hidden, span), BF16), V((X, hidden, span), BF16), V((X, span, hidden), BF16),
        V(gate_weight.shape, F32), V(up_weight.shape, F32), V(down_weight.shape, F32),
        V((2, X, ZH, Y, 16, T), BF16),
        V((3, CORES, ZL, part, T), F32),
        V((3, ZL, part, T), BF16), V((3, ZL, part, T), BF16),
        V((ZL, 3, part, T), BF16), V((ZL, 3, part, T), BF16),
        V((3, CORES, ZL, part, T), BF16),
        V((2, X, ZH, Y, 16, T), F32),
        V((2, 6, X, 16, T), BF16), V((2, 6, X, 16, T), BF16),
        V((2, 2, X // 2, 16, T), BF16), V((2, 2, X // 2, 16, T), BF16),
        V((2, X - 1, 16, T), BF16), V((2, X - 1, 16, T), BF16),
        V((2, 16, T), F32),
        V((2, X - 1, Y, 16, T), BF16), V((2, X - 1, Y, 16, T), BF16),
        V((2, Y, 16, T), BF16), V((2, Y, 16, T), BF16),
        V((2, 16, T), BF16), V((2, 16, T), BF16),
        pltpu.SemaphoreType.DMA((200,)),
        pltpu.SemaphoreType.DMA((200,)),
        pltpu.SemaphoreType.DMA((10,)),
    ]
    anywhere = pl.BlockSpec(memory_space=pl.ANY)
    S = jax.ShapeDtypeStruct
    shapes = (
        S((16, n), BF16), S((16, n), BF16),
        S(gate_weight.shape, F32), S(up_weight.shape, F32), S(down_weight.shape, F32),
    )
    outs = pl.pallas_call(
        kernel,
        out_shape=shapes,
        in_specs=[anywhere] * 5,
        out_specs=(anywhere,) * 5,
        scratch_shapes=scratch,
        compiler_params=pltpu.CompilerParams(
            collective_id=0, has_side_effects=True, vmem_limit_bytes=60 * 2**20
        ),
        cost_estimate=pl.CostEstimate(flops=18 * n * depth * hidden, bytes_accessed=18 * depth * hidden, transcendentals=0),
        name="ffn",
    )(tokens.T, cotangent.T, gate_weight, up_weight, down_weight)
    output, input_grad, *grads = pl.pallas_call(
        hand_on,
        out_shape=shapes,
        in_specs=[anywhere] * 5,
        out_specs=(anywhere,) * 5,
        scratch_shapes=[pltpu.SemaphoreType.DMA((5,))],
        name="hand_on",
    )(*outs)
    return (output.T, input_grad.T, *grads)


def solution(mesh):
    return jax.shard_map(
        body,
        mesh=mesh,
        in_specs=(
            P(None, ("width", "blk")),
            P("width", "blk"),
            P("width", "blk"),
            P("blk", "width"),
            P(None, ("width", "blk")),
        ),
        out_specs=(
            P(None, ("width", "blk")),
            P(None, ("width", "blk")),
            P("width", "blk"),
            P("width", "blk"),
            P("blk", "width"),
        ),
        check_vma=False,
    )
```

time: 2190 us -> 178 us (0.08)
  waiting for transfers between devices: 1750 us -> 0 us
  blocking collectives: 411 us -> 0 us
  Pallas kernels: 0 us -> 177 us
    reduce_scatter x2 -> x0, waiting for transfers between devices: 1630 us -> none  [the longest x1 821 us: body(): lax.psum_scatter(input_part, 'blk', scatter_dimension=1, tiled=True)]
    all_gather x2 -> x0, blocking collectives: 411 us -> none  [the longest x1 212 us: body(): grads_all = lax.all_gather(cotangent, 'blk', axis=1, tiled=True)]
    pallas_call x0 -> x2, Pallas kernels: none -> 177 us  [the longest x1 97.2 us: body(): pl.pallas_call(hand_on, out_shape=shapes, in_specs=[anywhere] * 5, out_sp...]
    psum x2 -> x0, waiting for transfers between devices: 111 us -> none  [the longest x1 111 us: body(): gate_pre, up_pre = lax.psum((gate_part, up_part), 'width')]
  transfers between devices with their start and end apart: 4 -> 0, of which waited for: 3 -> 0; matrix products, arithmetic and copies ran while one was open for 1% -> 0% of each run, Pallas kernels for 0% -> 0%
where the time goes in v2:
time: 178 us; the launch traced here: 177 us
  Pallas kernels  177 us (99%)
    pallas_call x1, Pallas kernels, body(): pl.pallas_call(hand_on, out_shape=shapes, in_specs=[anywhere] * 5, out_sp...  97.2 us
    pallas_call x1, Pallas kernels, body(): pl.pallas_call(kernel, out_shape=shapes, in_specs=[anywhere] * 5, out_spe...  79.4 us

profile of v2, /device:TPU:6, one launch (start us, length us, event | category | flops | bytes accessed | tf_op | source)
XLA Modules:
  0.0 177.2 jit_solution(17492418698706544806)
XLA Ops:
  0.6 79.4 %ffn.1 = (bf16[16,352]{1,0:T(8,128)(2,1)}, bf16[16,352]{1,0:T(8,128)(2,1)}, f32[1024,256]{1,0:T(8,128)}, f32[1024,256]{1,0:T(8,128)}, f32[256,1024]{1,0:T(8,128)}) custom-call(bf16[16,352]{1,0:T(8,128)(2,1)} %bitcast.4, bf16[16,352]{1,0:T(8,128)(2,1)} %bitcast.5, bf16[1024,256]{1,0:T(8,128)(2,1)} %gw_hbm.1, bf16[1024,256]{1,0:T(8,128)(2,1)} %uw_hbm.1, ...), custom_call_target="tpu_custom_call" | custom-call | flops 1660944384 | bytes 4718592 | tf_op jit(solution)/shard_map/ffn/pallas_call | solution.py:391
  80.1 97.2 %hand_on.1 = (bf16[16,352]{1,0:T(8,128)(2,1)}, bf16[16,352]{1,0:T(8,128)(2,1)}, f32[1024,256]{1,0:T(8,128)}, f32[1024,256]{1,0:T(8,128)}, f32[256,1024]{1,0:T(8,128)}) custom-call(bf16[16,352]{1,0:T(8,128)(2,1)} %get-tuple-element.15.refs_0_, bf16[16,352]{1,0:T(8,128)(2,1)} %get-tuple-element.16.refs_1_, f32[1024,256]{1,0:T(8,128)} %get-tuple-element.17.refs_2_, ...), custom_call_target="tpu_custom_call" | custom-call | tf_op jit(solution)/shard_map/hand_on/pallas_call | solution.py:403

commit v3 on v2

--- a/solution.py
+++ b/solution.py
@@ -347,11 +347,16 @@
 
 
 def hand_on(*refs):
-    n = len(refs) // 2
-    copies = [pltpu.make_async_copy(refs[i], refs[n + i], refs[-1].at[i]) for i in range(n)]
-    for c in copies:
+    n = (len(refs) - 1) // 3
+    src, dst, via, sem = refs[:n], refs[n : 2 * n], refs[2 * n : 3 * n], refs[-1]
+    ins = [pltpu.make_async_copy(src[i], via[i], sem.at[0, i]) for i in range(n)]
+    outs = [pltpu.make_async_copy(via[i], dst[i], sem.at[1, i]) for i in range(n)]
+    for c in ins:
         c.start()
-    for c in copies:
+    for i, c in enumerate(ins):
+        c.wait()
+        outs[i].start()
+    for c in outs:
         c.wait()
 
 
@@ -405,7 +410,8 @@
         out_shape=shapes,
         in_specs=[anywhere] * 5,
         out_specs=(anywhere,) * 5,
-        scratch_shapes=[pltpu.SemaphoreType.DMA((5,))],
+        scratch_shapes=[V(a.shape, a.dtype) for a in shapes] + [pltpu.SemaphoreType.DMA((2, len(shapes)))],
+        compiler_params=pltpu.CompilerParams(vmem_limit_bytes=60 * 2**20),
         name="hand_on",
     )(*outs)
     return (output.T, input_grad.T, *grads)

time: 178 us -> 83.8 us (0.47)
  Pallas kernels: 177 us -> 82.4 us
    pallas_call x1, Pallas kernels: 97.2 us -> 3.01 us  [body(): pl.pallas_call(hand_on, out_shape=shapes, in_specs=[anywhere] * 5, out_sp...]
where the time goes in v3:
time: 83.8 us; the launch traced here: 83.1 us
  Pallas kernels  82.4 us (98%)
    pallas_call x1, Pallas kernels, body(): pl.pallas_call(kernel, out_shape=shapes, in_specs=[anywhere] * 5, out_spe...  79.4 us
    pallas_call x1, Pallas kernels, body(): pl.pallas_call(hand_on, out_shape=shapes, in_specs=[anywhere] * 5, out_sp...  3.01 us

profile of v3, /device:TPU:6, one launch (start us, length us, event | category | flops | bytes accessed | tf_op | source)
XLA Modules:
  0.0 83.1 jit_solution(4373866043705161045)
XLA Ops:
  0.6 79.4 %ffn.1 = (bf16[16,352]{1,0:T(8,128)(2,1)}, bf16[16,352]{1,0:T(8,128)(2,1)}, f32[1024,256]{1,0:T(8,128)}, f32[1024,256]{1,0:T(8,128)}, f32[256,1024]{1,0:T(8,128)}) custom-call(bf16[16,352]{1,0:T(8,128)(2,1)} %bitcast.4, bf16[16,352]{1,0:T(8,128)(2,1)} %bitcast.5, bf16[1024,256]{1,0:T(8,128)(2,1)} %gw_hbm.1, bf16[1024,256]{1,0:T(8,128)(2,1)} %uw_hbm.1, ...), custom_call_target="tpu_custom_call" | custom-call | flops 1660944384 | bytes 4718592 | tf_op jit(solution)/shard_map/ffn/pallas_call | solution.py:396
  80.1 3.0 %hand_on.1 = (bf16[16,352]{1,0:T(8,128)(2,1)}, bf16[16,352]{1,0:T(8,128)(2,1)}, f32[1024,256]{1,0:T(8,128)}, f32[1024,256]{1,0:T(8,128)}, f32[256,1024]{1,0:T(8,128)}) custom-call(bf16[16,352]{1,0:T(8,128)(2,1)} %get-tuple-element.15.refs_0_, bf16[16,352]{1,0:T(8,128)(2,1)} %get-tuple-element.16.refs_1_, f32[1024,256]{1,0:T(8,128)} %get-tuple-element.17.refs_2_, ...), custom_call_target="tpu_custom_call" | custom-call | tf_op jit(solution)/shard_map/hand_on/pallas_call | solution.py:408

commit v4 on v3

--- a/solution.py
+++ b/solution.py
@@ -11,6 +11,7 @@
 X, ZH, Y = 4, 2, 8
 ZL, CORES = 4, 2
 F32, BF16 = jnp.float32, jnp.bfloat16
+FAR = (4, 3, -3, 2, -2, 1, -1, 0)
 
 
 def mm(left, right, dims):
@@ -32,22 +33,17 @@
         self.live.append(c)
         return c
 
-
-def turns(*gens):
-    gens = list(gens)
-    while gens:
-        for g in list(gens):
-            try:
-                next(g)
-            except StopIteration:
-                gens.remove(g)
+    def settle(self):
+        for c in self.live:
+            c.wait_send()
+        self.live = []
 
 
 def kernel(
     tok_hbm, cot_hbm, gw_hbm, uw_hbm, dw_hbm,
     out_hbm, inp_hbm, gwg_hbm, uwg_hbm, dwg_hbm,
-    io, gw, uw, dw, gwT, uwT, dwT, gwg, uwg, dwg, G, PF, P16, C1, SZ, RZ, H, OT,
-    SA, RA, SF, RF, SX, RX, ACC, SD, RD, SY, RY, SW, RW,
+    io, gw, uw, dw, wT, dwT, gwg, uwg, dwg, G, PF, P16, C1, SZ, RZ, H, OT,
+    SA, RA, SF, RF, SX, RX, ACC, SD, RD, SY, RY, SUM,
     send_sem, recv_sem, local_sem,
 ):
     b, w = lax.axis_index("blk"), lax.axis_index("width")
@@ -66,12 +62,12 @@
 
     xdev = {d: ((xs(d) * ZH + zh) * Y + y, w) for d in range(1, X)}
     ydev = {d: ((x * ZH + zh) * Y + ys(d), w) for d in (1, -1, 2, -2, 3, -3, 4)}
-    zdev = ((x * ZH + oz) * Y + y, w)
+    zdev = {d: ((x * ZH + oz) * Y + ys(d), w) for d in FAR}
     cdev = (b, zl * CORES + oc)
     ldev = {d: (b, ((zl + d) % ZL) * CORES + core) for d in range(1, ZL)}
 
     barrier = pltpu.get_barrier_semaphore()
-    partners = [zdev] + list(ldev.values()) + list(ydev.values()) + list(xdev.values()) + [cdev]
+    partners = list(zdev.values()) + list(ldev.values()) + list(ydev.values()) + list(xdev.values()) + [cdev]
     for p in partners:
         pl.semaphore_signal(barrier, inc=1, device_id=p, device_id_type=MESH)
 
@@ -86,13 +82,6 @@
     for t in range(2):
         loads[t].wait()
         G[t, 0, zh, y] = jnp.pad(io[t].astype(F32), ((0, 0), (0, T - tokens))).astype(BF16)
-    for c in loads[2:]:
-        c.wait()
-    for i in range(X):
-        s = slice(i * span, (i + 1) * span)
-        gwT[i] = gw[s, :].T
-        uwT[i] = uw[s, :].T
-        dwT[i] = dw[:, s].T
     pl.semaphore_wait(barrier, len(partners))
 
     sems = Sems(send_sem, recv_sem)
@@ -103,41 +92,32 @@
     def block(t, d):
         return G[t, d].reshape(span, T)
 
-    def part(t, d):
-        i = xs(-d)
-        v = block(t, d)
-        if t == 0:
-            new = (mm(gwT[i], v, (1, 0)), mm(uwT[i], v, (1, 0)))
-        else:
-            new = (mm(dw[:, cols(i)], v, (1, 0)),)
-        for n, p in enumerate(new):
-            p = p.reshape(PF.shape[1:])
-            PF[2 * t + n] = p if d == 0 else PF[2 * t + n] + p
-
-    def gather(t, zm):
+    def parts(t):
+        @pl.loop(0, X)
+        def _(d):
+            i = (x + X - d) % X
+            for n in range(2) if t == 0 else (2,):
+                left = wT[n, i] if t == 0 else dw[:, cols(i)]
+                PF[n] += mm(left, block(t, d), (1, 0)).reshape(PF.shape[1:])
+
+    def gather(t):
         own, rest = G.at[t, 0, zh, y], G.at[t, pl.ds(1, X - 1), zh, y]
-        near = (1, -1, 2, -2)
+        near = (2, -2, 1, -1)
         xm = {d: sems.copy(own, G.at[t, d, zh, y], xdev[d]) for d in (2, 1, 3)}
+        B = {e: sems.copy(own, own, zdev[e]) for e in FAR}
         N1 = {e: sems.copy(own, own, ydev[e]) for e in near}
+        XB, F = [], []
         yield
         for d in (1, 3, 2):
             xm[d].wait_recv()
-        N2 = {e: sems.copy(rest, rest, ydev[e]) for e in (2, -2, 1, -1)}
-        yield
-        if t == 0:
-            zm.wait_recv()
-        other = G.at[t, 0, oz, y]
-        B = {e: sems.copy(other, other, ydev[e]) for e in (1, -1, 2, -2, 3, -3, 4)}
-        XB = {}
-
-        def spread(e):
+        N2 = {e: sems.copy(rest, rest, ydev[e]) for e in near}
+        yield
+        for e in FAR:
+            B[e].wait_recv()
             piece = G.at[t, 0, oz, ys(-e)]
             for d in (2, 1, 3):
-                XB[e, d] = sems.copy(piece, G.at[t, d, oz, ys(-e)], xdev[d])
-
-        spread(0)
-        yield
-        F = []
+                XB.append(sems.copy(piece, G.at[t, d, oz, ys(-e)], xdev[d]))
+        yield
         for s, half in ((1, pl.ds(0, X // 2)), (-1, pl.ds(X // 2, X // 2))):
             N1[2 * s].wait_recv()
             N2[2 * s].wait_recv()
@@ -146,22 +126,12 @@
             piece = G.at[t, :, zh, ys(-2 * s)]
             F.append(sems.copy(piece, piece, ydev[s]))
         yield
-        for e in (1, -1, 2, -2, 3, -3, 4):
-            B[e].wait_recv()
-            spread(e)
-            if e != 1 and e != 2 and e != 3:
-                yield
         for e in (1, -1):
             N1[e].wait_recv()
             N2[e].wait_recv()
-        for c in F:
+        for c in F + XB:
             c.wait_recv()
-        part(t, 0)
-        yield
-        for d in (1, 3, 2):
-            for e in (0, 1, -1, 2, -2, 3, -3, 4):
-                XB[e, d].wait_recv()
-            part(t, d)
+        parts(t)
 
     def width_sum(a0, na, result):
         a = pl.ds(a0, na)
@@ -220,7 +190,6 @@
             SF[t, i] = OT[t, halves[s], zh, ys(4)].astype(BF16)
             F4[i] = sems.copy(SF.at[t, i], RF.at[t, i], ydev[2 * s])
             send(i, OT[t, :, zh, ys(3 * s)], ydev[s])
-        yield
         for i, s in enumerate((1, -1)):
             send(2 + i, OT[t, :, zh, ys(s)], ydev[s])
         yield
@@ -243,12 +212,11 @@
             ACC[t] += RX[t, d - 1].astype(F32)
 
     def scatter_b(t):
-        order = (4, -3, 3, -2, 2, -1, 1, 0)
         groups = ((0, 3), (3, 5), (5, 8))
-        D, M = {}, {}
+        D, M = {}, []
         for lo, hi in groups:
             for n in range(lo, hi):
-                SD[t, :, n] = OT[t, pl.ds(1, X - 1), oz, ys(order[n])].astype(BF16)
+                SD[t, :, n] = OT[t, pl.ds(1, X - 1), oz, ys(FAR[n])].astype(BF16)
             for d in (2, 1, 3):
                 at = (t, d - 1, pl.ds(lo, hi - lo))
                 D[lo, d] = sems.copy(SD.at[at], RD.at[at], xdev[d])
@@ -257,32 +225,36 @@
             for d in (1, 3, 2):
                 D[lo, d].wait_recv()
             for n in range(lo, hi):
-                v = OT[t, 0, oz, ys(order[n])]
+                v = OT[t, 0, oz, ys(FAR[n])]
                 for d in range(1, X):
                     v = v + RD[t, d - 1, n].astype(F32)
-                if order[n]:
-                    SY[t, n] = v.astype(BF16)
-                    M[n] = sems.copy(SY.at[t, n], RY.at[t, n], ydev[order[n]])
+                SY[t, n] = v.astype(BF16)
+                M.append(sems.copy(SY.at[t, n], RY.at[t, n], zdev[FAR[n]]))
             yield
-        for n in (5, 6, 3, 4, 1, 2, 0):
+        v = None
+        for n in range(Y):
             M[n].wait_recv()
-            v = v + RY[t, n].astype(F32)
-        SW[t] = v.astype(BF16)
-        M[7] = sems.copy(SW.at[t], RW.at[t], zdev)
-        yield
-        M[7].wait_recv()
+            v = RY[t, n].astype(F32) + (0.0 if v is None else v)
+        SUM[t] = v
 
     def hid(i):
         return H[i].reshape(dw.shape[0], T)
 
+    stores = []
+
+    def store(src, dst):
+        c = pltpu.make_async_copy(src, dst, local_sem.at[5 + len(stores)])
+        c.start()
+        stores.append(c)
+
     def grads():
-        for d in range(X):
-            i = xs(-d)
-            dwg[:, cols(i)] = mm(hid(0), block(1, d), (1, 1))
-            yield
-            gwg[cols(i), :] = mm(block(0, d), hid(1), (1, 1))
-            yield
-            uwg[cols(i), :] = mm(block(0, d), hid(2), (1, 1))
+        for n, (g, g_hbm) in enumerate(((gwg, gwg_hbm), (uwg, uwg_hbm))):
+
+            @pl.loop(0, X)
+            def _(d):
+                g[cols((x + X - d) % X), :] = mm(block(0, d), hid(1 + n), (1, 1))
+
+            store(g, g_hbm)
             yield
 
     def put(t, d, v):
@@ -292,17 +264,22 @@
         for _ in g:
             pass
 
-    both = G.at[:, 0, zh, y]
-    zm = sems.copy(both, both, zdev)
-    tok, cot = gather(0, zm), gather(1, zm)
-    left = True
-    while left:
-        left = False
-        for _ in tok:
-            left = True
-            break
-        if left:
-            next(cot)
+    tok, cot = gather(0), gather(1)
+    next(tok)
+    next(cot)
+    for c in loads[2:]:
+        c.wait()
+    PF[...] = jnp.zeros_like(PF)
+
+    @pl.loop(0, X)
+    def _(i):
+        wT[0, i] = gw[cols(i), :].T
+        wT[1, i] = uw[cols(i), :].T
+        dwT[i] = dw[:, cols(i)].T
+
+    for g in (tok, cot, tok, tok, cot, cot):
+        next(g)
+    drain(tok)
     pre = width_sum(0, 2, make_hidden)
     next(pre)
     next(pre)
@@ -310,6 +287,7 @@
     post = width_sum(2, 1, make_grads)
     next(post)
     next(post)
+    sems.settle()
     drain(pre)
     fore = width_gather(0, 1)
     next(fore)
@@ -317,30 +295,35 @@
     back = width_gather(1, 2)
     next(back)
     drain(fore)
-    for d in range(X):
-        put(0, d, mm(dwT[xs(d)], hid(0), (1, 0)))
-    out = [scatter_b(0), scatter_a(0)]
-    for g in out:
+
+    @pl.loop(0, X)
+    def _(d):
+        put(0, d, mm(dwT[(x + d) % X], hid(0), (1, 0)))
+
+    b0, a0, b1, a1, dw_up = scatter_b(0), scatter_a(0), scatter_b(1), scatter_a(1), grads()
+    next(b0)
+    next(a0)
+
+    @pl.loop(0, X)
+    def _(d):
+        dwg[:, cols((x + X - d) % X)] = mm(hid(0), block(1, d), (1, 1))
+
+    store(dwg, dwg_hbm)
+    drain(back)
+
+    @pl.loop(0, X)
+    def _(d):
+        i = (x + d) % X
+        put(1, d, mm(gw[cols(i), :], hid(1), (1, 0)) + mm(uw[cols(i), :], hid(2), (1, 0)))
+
+    for g in (b1, a1, b0, a0, b0, b0, b1, a1, b1, b1, dw_up, a0, dw_up, a1):
         next(g)
-    drain(back)
-    for d in range(X):
-        i = xs(d)
-        put(1, d, mm(gw[cols(i), :], hid(1), (1, 0)) + mm(uw[cols(i), :], hid(2), (1, 0)))
-    turns(scatter_b(1), scatter_a(1), *out, grads())
-    stores = []
-
-    def store(src, dst):
-        c = pltpu.make_async_copy(src, dst, local_sem.at[5 + len(stores)])
-        c.start()
-        stores.append(c)
-
-    for src, dst in ((dwg, dwg_hbm), (gwg, gwg_hbm), (uwg, uwg_hbm)):
-        store(src, dst)
+    for g in (dw_up, b0, a0, a1, b1):
+        drain(g)
     for t, ref in enumerate((out_hbm, inp_hbm)):
-        io[t] = (ACC[t] + RW[t].astype(F32)).astype(BF16)[:, :tokens]
+        io[t] = (ACC[t] + SUM[t]).astype(BF16)[:, :tokens]
         store(io.at[t], ref)
-    for c in sems.live:
-        c.wait_send()
+    sems.settle()
     for c in stores:
         c.wait()
     assert sems.used <= send_sem.shape[0], sems.used
@@ -368,7 +351,7 @@
     scratch = [
         V((2, 16, n), BF16),
         V(gate_weight.shape, BF16), V(up_weight.shape, BF16), V(down_weight.shape, BF16),
-        V((X, hidden, span), BF16), V((X, hidden, span), BF16), V((X, span, hidden), BF16),
+        V((2, X, hidden, span), BF16), V((X, span, hidden), BF16),
         V(gate_weight.shape, F32), V(up_weight.shape, F32), V(down_weight.shape, F32),
         V((2, X, ZH, Y, 16, T), BF16),
         V((3, CORES, ZL, part, T), F32),
@@ -382,7 +365,7 @@
         V((2, 16, T), F32),
         V((2, X - 1, Y, 16, T), BF16), V((2, X - 1, Y, 16, T), BF16),
         V((2, Y, 16, T), BF16), V((2, Y, 16, T), BF16),
-        V((2, 16, T), BF16), V((2, 16, T), BF16),
+        V((2, 16, T), F32),
         pltpu.SemaphoreType.DMA((200,)),
         pltpu.SemaphoreType.DMA((200,)),
         pltpu.SemaphoreType.DMA((10,)),

time: 83.8 us -> 78.2 us (0.933)
  Pallas kernels: 82.4 us -> 76.7 us
    pallas_call x1, Pallas kernels: 79.4 us -> 73.7 us  [body(): pl.pallas_call(kernel, out_shape=shapes, in_specs=[anywhere] * 5, out_spe...]
where the time goes in v4:
time: 78.2 us; the launch traced here: 77.3 us
  Pallas kernels  76.7 us (98%)
    pallas_call x1, Pallas kernels, body(): pl.pallas_call(kernel, out_shape=shapes, in_specs=[anywhere] * 5, out_spe...  73.7 us
    pallas_call x1, Pallas kernels, body(): pl.pallas_call(hand_on, out_shape=shapes, in_specs=[anywhere] * 5, out_sp...  3.01 us

profile of v4, /device:TPU:6, one launch (start us, length us, event | category | flops | bytes accessed | tf_op | source)
XLA Modules:
  0.0 77.3 jit_solution(4364054949822788970)
XLA Ops:
  0.6 73.7 %ffn.1 = (bf16[16,352]{1,0:T(8,128)(2,1)}, bf16[16,352]{1,0:T(8,128)(2,1)}, f32[1024,256]{1,0:T(8,128)}, f32[1024,256]{1,0:T(8,128)}, f32[256,1024]{1,0:T(8,128)}) custom-call(bf16[16,352]{1,0:T(8,128)(2,1)} %bitcast.4, bf16[16,352]{1,0:T(8,128)(2,1)} %bitcast.5, bf16[1024,256]{1,0:T(8,128)(2,1)} %gw_hbm.1, bf16[1024,256]{1,0:T(8,128)(2,1)} %uw_hbm.1, ...), custom_call_target="tpu_custom_call" | custom-call | flops 1660944384 | bytes 4718592 | tf_op jit(solution)/shard_map/ffn/pallas_call | solution.py:379
  74.3 3.0 %hand_on.1 = (bf16[16,352]{1,0:T(8,128)(2,1)}, bf16[16,352]{1,0:T(8,128)(2,1)}, f32[1024,256]{1,0:T(8,128)}, f32[1024,256]{1,0:T(8,128)}, f32[256,1024]{1,0:T(8,128)}) custom-call(bf16[16,352]{1,0:T(8,128)(2,1)} %get-tuple-element.15.refs_0_, bf16[16,352]{1,0:T(8,128)(2,1)} %get-tuple-element.16.refs_1_, f32[1024,256]{1,0:T(8,128)} %get-tuple-element.17.refs_2_, ...), custom_call_target="tpu_custom_call" | custom-call | tf_op jit(solution)/shard_map/hand_on/pallas_call | solution.py:391

commit v5 on v4

--- a/solution.py
+++ b/solution.py
@@ -8,6 +8,7 @@
 from jax.sharding import PartitionSpec as P
 
 MESH = pl.DeviceIdType.MESH
+PIECES = 4
 X, ZH, Y = 4, 2, 8
 ZL, CORES = 4, 2
 F32, BF16 = jnp.float32, jnp.bfloat16
@@ -101,16 +102,15 @@
                 PF[n] += mm(left, block(t, d), (1, 0)).reshape(PF.shape[1:])
 
     def gather(t):
-        own, rest = G.at[t, 0, zh, y], G.at[t, pl.ds(1, X - 1), zh, y]
+        own, line = G.at[t, 0, zh, y], G.at[t, :, zh, y]
         near = (2, -2, 1, -1)
         xm = {d: sems.copy(own, G.at[t, d, zh, y], xdev[d]) for d in (2, 1, 3)}
         B = {e: sems.copy(own, own, zdev[e]) for e in FAR}
-        N1 = {e: sems.copy(own, own, ydev[e]) for e in near}
         XB, F = [], []
         yield
         for d in (1, 3, 2):
             xm[d].wait_recv()
-        N2 = {e: sems.copy(rest, rest, ydev[e]) for e in near}
+        N = {e: sems.copy(line, line, ydev[e]) for e in near}
         yield
         for e in FAR:
             B[e].wait_recv()
@@ -119,16 +119,14 @@
                 XB.append(sems.copy(piece, G.at[t, d, oz, ys(-e)], xdev[d]))
         yield
         for s, half in ((1, pl.ds(0, X // 2)), (-1, pl.ds(X // 2, X // 2))):
-            N1[2 * s].wait_recv()
-            N2[2 * s].wait_recv()
+            N[2 * s].wait_recv()
             piece = G.at[t, half, zh, ys(-2 * s)]
             F.append(sems.copy(piece, piece, ydev[2 * s]))
             piece = G.at[t, :, zh, ys(-2 * s)]
             F.append(sems.copy(piece, piece, ydev[s]))
         yield
         for e in (1, -1):
-            N1[e].wait_recv()
-            N2[e].wait_recv()
+            N[e].wait_recv()
         for c in F + XB:
             c.wait_recv()
         parts(t)
@@ -212,7 +210,7 @@
             ACC[t] += RX[t, d - 1].astype(F32)
 
     def scatter_b(t):
-        groups = ((0, 3), (3, 5), (5, 8))
+        groups = ((0, 4), (4, 8))
         D, M = {}, []
         for lo, hi in groups:
             for n in range(lo, hi):
@@ -316,9 +314,10 @@
         i = (x + d) % X
         put(1, d, mm(gw[cols(i), :], hid(1), (1, 0)) + mm(uw[cols(i), :], hid(2), (1, 0)))
 
-    for g in (b1, a1, b0, a0, b0, b0, b1, a1, b1, b1, dw_up, a0, dw_up, a1):
+    for g in (b1, a1, b0, a0, b0, b1, a1, b1, dw_up, a0, dw_up, a1):
         next(g)
-    for g in (dw_up, b0, a0, a1, b1):
+    sems.settle()
+    for g in (dw_up, a0, b0, a1, b1):
         drain(g)
     for t, ref in enumerate((out_hbm, inp_hbm)):
         io[t] = (ACC[t] + SUM[t]).astype(BF16)[:, :tokens]
@@ -332,8 +331,14 @@
 def hand_on(*refs):
     n = (len(refs) - 1) // 3
     src, dst, via, sem = refs[:n], refs[n : 2 * n], refs[2 * n : 3 * n], refs[-1]
-    ins = [pltpu.make_async_copy(src[i], via[i], sem.at[0, i]) for i in range(n)]
-    outs = [pltpu.make_async_copy(via[i], dst[i], sem.at[1, i]) for i in range(n)]
+    ins, outs = [], []
+    for i in range(n):
+        rows = src[i].shape[0]
+        step = max(16, rows // PIECES)
+        for at in range(0, rows, step):
+            s, k = pl.ds(at, step), len(ins)
+            ins.append(pltpu.make_async_copy(src[i].at[s], via[i].at[s], sem.at[0, k]))
+            outs.append(pltpu.make_async_copy(via[i].at[s], dst[i].at[s], sem.at[1, k]))
     for c in ins:
         c.start()
     for i, c in enumerate(ins):
@@ -393,7 +398,7 @@
         out_shape=shapes,
         in_specs=[anywhere] * 5,
         out_specs=(anywhere,) * 5,
-        scratch_shapes=[V(a.shape, a.dtype) for a in shapes] + [pltpu.SemaphoreType.DMA((2, len(shapes)))],
+        scratch_shapes=[V(a.shape, a.dtype) for a in shapes] + [pltpu.SemaphoreType.DMA((2, PIECES * len(shapes)))],
         compiler_params=pltpu.CompilerParams(vmem_limit_bytes=60 * 2**20),
         name="hand_on",
     )(*outs)

time: 78.2 us -> 77.4 us (0.990)
  Pallas kernels: 76.7 us -> 75.6 us
    pallas_call x1, Pallas kernels: 73.7 us -> 72.6 us  [body(): pl.pallas_call(kernel, out_shape=shapes, in_specs=[anywhere] * 5, out_spe...]
where the time goes in v5:
time: 77.4 us; the launch traced here: 76.2 us
  Pallas kernels  75.6 us (98%)
    pallas_call x1, Pallas kernels, body(): pl.pallas_call(kernel, out_shape=shapes, in_specs=[anywhere] * 5, out_spe...  72.6 us
    pallas_call x1, Pallas kernels, body(): pl.pallas_call(hand_on, out_shape=shapes, in_specs=[anywhere] * 5, out_sp...  2.99 us

profile of v5, /device:TPU:6, one launch (start us, length us, event | category | flops | bytes accessed | tf_op | source)
XLA Modules:
  0.0 76.2 jit_solution(8810599580261345860)
XLA Ops:
  0.6 72.6 %ffn.1 = (bf16[16,352]{1,0:T(8,128)(2,1)}, bf16[16,352]{1,0:T(8,128)(2,1)}, f32[1024,256]{1,0:T(8,128)}, f32[1024,256]{1,0:T(8,128)}, f32[256,1024]{1,0:T(8,128)}) custom-call(bf16[16,352]{1,0:T(8,128)(2,1)} %bitcast.4, bf16[16,352]{1,0:T(8,128)(2,1)} %bitcast.5, bf16[1024,256]{1,0:T(8,128)(2,1)} %gw_hbm.1, bf16[1024,256]{1,0:T(8,128)(2,1)} %uw_hbm.1, ...), custom_call_target="tpu_custom_call" | custom-call | flops 1660944384 | bytes 4718592 | tf_op jit(solution)/shard_map/ffn/pallas_call | solution.py:384
  73.3 3.0 %hand_on.1 = (bf16[16,352]{1,0:T(8,128)(2,1)}, bf16[16,352]{1,0:T(8,128)(2,1)}, f32[1024,256]{1,0:T(8,128)}, f32[1024,256]{1,0:T(8,128)}, f32[256,1024]{1,0:T(8,128)}) custom-call(bf16[16,352]{1,0:T(8,128)(2,1)} %get-tuple-element.15.refs_0_, bf16[16,352]{1,0:T(8,128)(2,1)} %get-tuple-element.16.refs_1_, f32[1024,256]{1,0:T(8,128)} %get-tuple-element.17.refs_2_, ...), custom_call_target="tpu_custom_call" | custom-call | tf_op jit(solution)/shard_map/hand_on/pallas_call | solution.py:396

commit v6 on v5

--- a/solution.py
+++ b/solution.py
@@ -265,7 +265,7 @@
     tok, cot = gather(0), gather(1)
     next(tok)
     next(cot)
-    for c in loads[2:]:
+    for c in loads[2:4]:
         c.wait()
     PF[...] = jnp.zeros_like(PF)
 
@@ -273,8 +273,8 @@
     def _(i):
         wT[0, i] = gw[cols(i), :].T
         wT[1, i] = uw[cols(i), :].T
-        dwT[i] = dw[:, cols(i)].T
-
+
+    loads[4].wait()
     for g in (tok, cot, tok, tok, cot, cot):
         next(g)
     drain(tok)
@@ -285,6 +285,11 @@
     post = width_sum(2, 1, make_grads)
     next(post)
     next(post)
+
+    @pl.loop(0, X)
+    def _(i):
+        dwT[i] = dw[:, cols(i)].T
+
     sems.settle()
     drain(pre)
     fore = width_gather(0, 1)

time: 77.4 us -> 77.4 us (level)
  no operation moved by 1% of the time
where the time goes in v6:
time: 77.4 us; the launch traced here: 76.2 us
  Pallas kernels  75.6 us (98%)
    pallas_call x1, Pallas kernels, body(): pl.pallas_call(kernel, out_shape=shapes, in_specs=[anywhere] * 5, out_spe...  72.6 us
    pallas_call x1, Pallas kernels, body(): pl.pallas_call(hand_on, out_shape=shapes, in_specs=[anywhere] * 5, out_sp...  2.99 us

profile of v6, /device:TPU:6, one launch (start us, length us, event | category | flops | bytes accessed | tf_op | source)
XLA Modules:
  0.0 76.2 jit_solution(8980628027013568074)
XLA Ops:
  0.6 72.6 %ffn.1 = (bf16[16,352]{1,0:T(8,128)(2,1)}, bf16[16,352]{1,0:T(8,128)(2,1)}, f32[1024,256]{1,0:T(8,128)}, f32[1024,256]{1,0:T(8,128)}, f32[256,1024]{1,0:T(8,128)}) custom-call(bf16[16,352]{1,0:T(8,128)(2,1)} %bitcast.4, bf16[16,352]{1,0:T(8,128)(2,1)} %bitcast.5, bf16[1024,256]{1,0:T(8,128)(2,1)} %gw_hbm.1, bf16[1024,256]{1,0:T(8,128)(2,1)} %uw_hbm.1, ...), custom_call_target="tpu_custom_call" | custom-call | flops 1660944384 | bytes 4718592 | tf_op jit(solution)/shard_map/ffn/pallas_call | solution.py:389
  73.3 3.0 %hand_on.1 = (bf16[16,352]{1,0:T(8,128)(2,1)}, bf16[16,352]{1,0:T(8,128)(2,1)}, f32[1024,256]{1,0:T(8,128)}, f32[1024,256]{1,0:T(8,128)}, f32[256,1024]{1,0:T(8,128)}) custom-call(bf16[16,352]{1,0:T(8,128)(2,1)} %get-tuple-element.15.refs_0_, bf16[16,352]{1,0:T(8,128)(2,1)} %get-tuple-element.16.refs_1_, f32[1024,256]{1,0:T(8,128)} %get-tuple-element.17.refs_2_, ...), custom_call_target="tpu_custom_call" | custom-call | tf_op jit(solution)/shard_map/hand_on/pallas_call | solution.py:401
